TPU v7x, 32 devices: a whole 2x2x4 slice. The times are simulated.
32 devices in a mesh: row: 16 (over z, y, core), col: 2 (over x).
Axes of the slice: x: 2, y: 2, z: 4, core: 2. Of those that a mesh axis runs over, the one named last changes fastest.
Arguments:
- rhs: bfloat16 [262144, 128], P(('row', 'col')), may hold values from -6 to 6
- leaf_basis: bfloat16 [2048, 64, 256], P(('row', 'col')), may hold values from -0.375 to 0.375
- transfer: bfloat16 [4, 16, 2, 64, 64, 256], P(None, 'row', 'col'), may hold values from -0.375 to 0.375
- ranks: int32 [4, 16, 2, 64], P(None, 'row', 'col'), may hold values from 32 to 64, as said below
- out_basis: bfloat16 [16, 64, 128, 128], P('row'), may hold values from -0.375 to 0.375
Outputs:
- result: bfloat16 [131072, 128], P(('row', 'col'))
Inputs may be any that keep to these rules, and one draw needn't show every extreme that they name: `ranks`: at every level some block has live rank exactly 64.
All inputs are finite; a program needn't handle non-finite values.
Results may differ from a plain program's by a relative error of at most 0.0014.
Values sent between devices are 32-bit elements; how exact they have to be, the bound alone decides.
A program may use at most 128 MiB of HBM per device.

v0:
```python
import jax
import jax.numpy as jnp
from jax import lax
from jax.sharding import PartitionSpec as P


def from_partner(block, axis, bit):
    count = lax.axis_size(axis)
    route = []
    for low in range(count):
        high = low | 1 << bit
        if high != low and high < count:
            route += [(low, high), (high, low)]
    return lax.ppermute(block, axis, route)


def complex_stack(block):
    middle = block.shape[-1] // 2
    flipped = jnp.concatenate([-block[..., middle:], block[..., :middle]], -1)
    return jnp.concatenate([block, flipped], -2)


def mix_level(coeff, matrices, live_ranks, level, position):
    leaves = coeff.shape[0]
    rank_cap = coeff.shape[1]
    columns = coeff.shape[2]
    half_count = leaves // 2
    upper_bit = position >> level & 1
    kept_half = lax.dynamic_slice_in_dim(coeff, upper_bit * half_count, half_count, 0)
    sent_half = lax.dynamic_slice_in_dim(coeff, (1 - upper_bit) * half_count, half_count, 0)
    partner_half = from_partner(sent_half, "row", level)
    stacked = jnp.concatenate([complex_stack(kept_half), complex_stack(partner_half)], 1)
    weights = matrices.astype(jnp.float32).reshape(half_count, 2, rank_cap, 4 * rank_cap)
    mixed = jnp.einsum("jskm,jmn->jskn", weights, stacked, precision=lax.Precision.HIGHEST)
    mixed = mixed.reshape(leaves, rank_cap, columns)
    live_rows = jnp.arange(rank_cap, dtype=jnp.int32)[None, :] < live_ranks[:, None]
    return jnp.where(live_rows[..., None], mixed, jnp.float32(0.0))


def shards(rhs, leaf_basis, transfer, ranks, out_basis):
    leaves = leaf_basis.shape[0]
    points = leaf_basis.shape[2] // 2
    columns = rhs.shape[1]
    sources = rhs.reshape(leaves, points, columns)
    coeff = jnp.einsum(
        "gkm,gmn->gkn", leaf_basis, complex_stack(sources), preferred_element_type=jnp.float32
    )
    position = lax.axis_index("row")
    for level in range(transfer.shape[0]):
        coeff = mix_level(coeff, transfer[level, 0, 0], ranks[level, 0, 0], level, position)
    owned = leaves // lax.axis_size("col")
    targets = out_basis[0]
    total = lax.psum_scatter(coeff, "col", scatter_dimension=0, tiled=True)
    basis = lax.dynamic_slice_in_dim(targets, lax.axis_index("col") * owned, owned, 0).astype(
        jnp.float32
    )
    product = jnp.einsum(
        "glm,gmn->gln", basis, complex_stack(total), precision=lax.Precision.HIGHEST
    )
    result = product.reshape(owned * points, columns)
    return result.astype(jnp.bfloat16)


def solution(mesh):
    in_specs = (
        P(("row", "col"), None),
        P(("row", "col"), None, None),
        P(None, "row", "col", None, None, None),
        P(None, "row", "col", None),
        P("row", None, None, None),
    )
    out_specs = P(("row", "col"), None)
    return jax.shard_map(shards, mesh=mesh, in_specs=in_specs, out_specs=out_specs, check_vma=False)
```

profile of v0, /device:TPU:0, one launch (start us, length us, event | category | flops | bytes accessed | tf_op | source)
XLA Modules:
  0.0 196.9 jit_solution(10461350367729453149)
XLA Ops:
  6.5 0.0 copy-start
  6.5 0.0 reduce-scatter.2.cloned.1.call-start
  6.5 5.2 %slice_negate_fusion = (bf16[64,128,64]{2,1,0:T(8,128)(2,1)}, bf16[64,128,64]{2,1,0:T(8,128)(2,1)}) fusion(bf16[64,128,128]{2,1,0:T(8,128)(2,1)} %bitcast.62), kind=kLoop, calls=%fused_computation.54 | loop fusion | flops 524288 | bytes 4194304 | tf_op jit(solution)/shard_map/neg | solution.py:19
  11.7 3.9 %fusion = f32[64,128,64]{1,2,0:T(8,128)S(1)} fusion(bf16[64,64,256]{2,1,0:T(8,128)(2,1)S(1)} %copy-done, bf16[64,128,64]{2,1,0:T(8,128)(2,1)} %get-tuple-element.24, bf16[64,128,64]{2,1,0:T(8,128)(2,1)} %get-tuple-element.23, bf16[64,128,128]{2,1,0:T(8,128)(2,1)} %bitcast.63), kind=kOutput, calls=%fused_computation | convolution fusion | flops 281018368 | bytes 8388608 | tf_op jit(solution)/shard_map/gkm,gmn->gkn/dot_general | solution.py:45
  15.6 0.0 copy-start.9
  15.6 0.2 dynamic-slice_bitcast_fusion.1
  15.8 0.5 collective-permute-start
  16.3 0.1 iota_compare_fusion
  16.4 0.4 slice_negate_fusion.6
  16.8 5.6 %fusion.68 = (bf16[1,1,1,64,64,256]{5,4,3,2,1,0:T(8,128)(2,1)S(1)}, bf16[1,1,1,64,64,256]{5,4,3,2,1,0:T(8,128)(2,1)}, bf16[1,1,1,64,64,256]{5,4,3,2,1,0:T(8,128)(2,1)}, bf16[1,1,1,64,64,256]{5,4,3,2,1,0:T(8,128)(2,1)}) fusion(bf16[4,1,1,64,64,256]{5,4,3,2,1,0:T(8,128)(2,1)} %param.7), kind=kLoop, calls=%fused_computation.103 | loop fusion | bytes 16777216 | tf_op jit(solution)/shard_map/slice | solution.py:50
  22.4 0.0 collective-permute-done
  22.4 1.3 slice_negate_fusion.5
  23.8 4.6 %fusion.6 = f32[32,128,2,64]{1,3,2,0:T(8,128)S(1)} fusion(bf16[32,2,64,256]{3,2,1,0:T(8,128)(2,1)S(1)} %bitcast.67, f32[32,64,64]{2,1,0:T(8,128)} %get-tuple-element.36, f32[32,64,64]{2,1,0:T(8,128)S(1)} %get-tuple-element.35, f32[32,64,128]{2,1,0:T(8,128)S(1)} %collective-permute-done, f32[32,64,64]{2,1,0:T(8,128)S(1)} %get-tuple-element.34, ...), kind=kOutput, calls=%fused_computation.7 | convolution fusion | flops 1615855616 | bytes 8388608 | tf_op jit(solution)/shard_map/jskm,jmn->jskn/dot_general | solution.py:34
  28.4 0.9 bitcast_select_fusion.3
  29.2 1.6 constant_dynamic-slice_fusion.8
  30.8 2.9 %collective-permute-start.1 = (f32[32,64,128]{2,1,0:T(8,128)}, f32[32,64,128]{2,1,0:T(8,128)S(1)}, u32[]{:S(2)}, u32[]{:S(2)}) collective-permute-start(f32[32,64,128]{2,1,0:T(8,128)} %get-tuple-element.18), channel_id=1, source_target_pairs={{0,4},{4,0},{2,6},{6,2},{8,12},{12,8},{10,14},{14,10},{16,20},{20,... | collective-permute-start | bytes 3145736 | tf_op jit(solution)/shard_map/ppermute | solution.py:14
  33.7 0.1 iota_compare_fusion.1
  33.8 0.4 dynamic-slice_negate_fusion.2
  34.2 0.0 copy-start.6
  34.2 23.1 %collective-permute-done.1 = f32[32,64,128]{2,1,0:T(8,128)S(1)} collective-permute-done((f32[32,64,128]{2,1,0:T(8,128)}, f32[32,64,128]{2,1,0:T(8,128)S(1)}, u32[]{:S(2)}, u32[]{:S(2)}) %collective-permute-start.1) | collective-permute-done | bytes 1048608 | tf_op jit(solution)/shard_map/ppermute | solution.py:14
  57.4 1.3 slice_negate_fusion.4
  58.7 4.5 %fusion.17 = f32[32,128,2,64]{1,3,2,0:T(8,128)S(1)} fusion(bf16[32,2,64,256]{3,2,1,0:T(8,128)(2,1)S(1)} %bitcast.66, f32[32,64,64]{2,1,0:T(8,128)} %get-tuple-element.32, f32[32,64,64]{2,1,0:T(8,128)S(1)} %get-tuple-element.31, f32[32,64,128]{2,1,0:T(8,128)S(1)} %collective-permute-done.1, f32[32,64,64]{2,1,0:T(8,128)S(1)} %get-tuple-element.20, ...), kind=kOutput, calls=%fused_computation.19 | convolution fusion | flops 1615855616 | bytes 8388608 | tf_op jit(solution)/shard_map/jskm,jmn->jskn/dot_general | solution.py:34
  63.2 0.9 bitcast_select_fusion.2
  64.1 1.6 constant_dynamic-slice_fusion.6
  65.7 1.8 collective-permute-start.2
  67.5 0.1 iota_compare_fusion.2
  67.6 0.4 dynamic-slice_negate_fusion.1
  68.0 0.0 copy-start.7
  68.0 22.6 %collective-permute-done.2 = f32[32,64,128]{2,1,0:T(8,128)S(1)} collective-permute-done((f32[32,64,128]{2,1,0:T(8,128)}, f32[32,64,128]{2,1,0:T(8,128)S(1)}, u32[]{:S(2)}, u32[]{:S(2)}) %collective-permute-start.2) | collective-permute-done | bytes 1048608 | tf_op jit(solution)/shard_map/ppermute | solution.py:14
  90.6 1.4 slice_negate_fusion.3
  92.0 0.0 copy-done.7
  92.0 4.5 %fusion.28 = f32[32,128,2,64]{1,3,2,0:T(8,128)S(1)} fusion(bf16[32,2,64,256]{3,2,1,0:T(8,128)(2,1)S(1)} %bitcast.65, f32[32,64,64]{2,1,0:T(8,128)} %get-tuple-element.30, f32[32,64,64]{2,1,0:T(8,128)S(1)} %get-tuple-element.29, f32[32,64,128]{2,1,0:T(8,128)S(1)} %collective-permute-done.2, f32[32,64,64]{2,1,0:T(8,128)S(1)} %get-tuple-element.16, ...), kind=kOutput, calls=%fused_computation.31 | convolution fusion | flops 1615855616 | bytes 8388608 | tf_op jit(solution)/shard_map/jskm,jmn->jskn/dot_general | solution.py:34
  96.5 0.9 bitcast_select_fusion.1
  97.4 0.2 constant_dynamic-slice_fusion.4
  97.6 2.6 %collective-permute-start.3 = (f32[32,64,128]{2,1,0:T(8,128)S(1)}, f32[32,64,128]{2,1,0:T(8,128)S(1)}, u32[]{:S(2)}, u32[]{:S(2)}) collective-permute-start(f32[32,64,128]{2,1,0:T(8,128)S(1)} %get-tuple-element.10), channel_id=1, source_target_pairs={{0,16},{16,0},{2,18},{18,2},{4,20},{20,4},{6,22},{22,6},{8,24},{24... | collective-permute-start | bytes 3145736 | tf_op jit(solution)/shard_map/ppermute | solution.py:14
  100.2 0.1 iota_compare_fusion.3
  100.3 0.4 dynamic-slice_negate_fusion
  100.7 44.1 %collective-permute-done.3 = f32[32,64,128]{2,1,0:T(8,128)S(1)} collective-permute-done((f32[32,64,128]{2,1,0:T(8,128)S(1)}, f32[32,64,128]{2,1,0:T(8,128)S(1)}, u32[]{:S(2)}, u32[]{:S(2)}) %collective-permute-start.3) | collective-permute-done | bytes 1048608 | tf_op jit(solution)/shard_map/ppermute | solution.py:14
  144.8 1.4 slice_negate_fusion.2
  146.2 0.0 copy-done.3
  146.2 4.4 %fusion.39 = f32[32,128,2,64]{1,3,2,0:T(8,128)S(1)} fusion(bf16[32,2,64,256]{3,2,1,0:T(8,128)(2,1)S(1)} %bitcast.64, f32[32,64,64]{2,1,0:T(8,128)} %get-tuple-element.28, f32[32,64,64]{2,1,0:T(8,128)S(1)} %get-tuple-element.27, f32[32,64,128]{2,1,0:T(8,128)S(1)} %collective-permute-done.3, f32[32,64,64]{2,1,0:T(8,128)S(1)} %get-tuple-element.12, ...), kind=kOutput, calls=%fused_computation.43 | convolution fusion | flops 1615855616 | bytes 8388608 | tf_op jit(solution)/shard_map/jskm,jmn->jskn/dot_general | solution.py:34
  150.6 1.9 bitcast_select_fusion
  152.4 0.0 reduce-scatter.2.cloned.1.call-update
  152.5 32.7 %reduce-scatter.2.cloned.1.call-done = f32[32,64,128]{2,1,0:T(8,128)} async-done(((f32[64,64,128]{2,1,0:T(8,128)}), f32[32,64,128]{2,1,0:T(8,128)}) %reduce-scatter.2.cloned.1.call-update) | async-done | bytes 1048592 | tf_op jit(solution)/shard_map/reduce_scatter | solution.py:53
  185.2 2.1 %slice_negate_fusion.1 = (f32[32,64,64]{2,1,0:T(8,128)S(1)}, f32[32,64,64]{2,1,0:T(8,128)S(1)}) fusion(f32[32,64,128]{2,1,0:T(8,128)} %reduce-scatter.2.cloned.1.call-done), kind=kLoop, calls=%fused_computation.66 | loop fusion | flops 131072 | bytes 2097152 | tf_op jit(solution)/shard_map/neg | solution.py:19
  187.3 0.0 copy-start.1
  187.3 0.4 copy-done.8
  187.7 2.3 %fusion.56 = bf16[32,128,128]{2,1,0:T(8,128)(2,1)} fusion(f32[32,64,64]{2,1,0:T(8,128)S(1)} %get-tuple-element.26, f32[32,64,64]{2,1,0:T(8,128)S(1)} %get-tuple-element.25, f32[32,64,128]{2,1,0:T(8,128)S(1)} %copy-done.2, bf16[1,64,128,128]{3,2,1,0:T(8,128)(2,1)S(1)} %copy-done.8, s32[]{:T(128)S(6)} %select_n.40), kind=kOutput, calls=%fused_computation.65 | convolution fusion | flops 806879232 | bytes 5242884 | tf_op jit(solution)/shard_map/glm,gmn->gln/dot_general | solution.py:57
  (13 shorter events, 0.0 us)
Async XLA Ops:
  6.5 5.2 %copy-start = (bf16[64,64,256]{2,1,0:T(8,128)(2,1)S(1)}, bf16[64,64,256]{2,1,0:T(8,128)(2,1)}, u32[]{:S(2)}) copy-start(bf16[64,64,256]{2,1,0:T(8,128)(2,1)} %param.6) | copy-start | bytes 6291460
  6.5 178.6 %reduce-scatter.2.cloned.1.call-start = ((), (), s32[]{:S(2)}) async-start(), calls=%async_computation.1 | async-start | bytes 3145728 | tf_op jit(solution)/shard_map/reduce_scatter | solution.py:53
  15.6 0.7 copy-start.9
  15.8 6.6 %collective-permute-start = (f32[32,64,128]{2,1,0:T(8,128)S(1)}, f32[32,64,128]{2,1,0:T(8,128)S(1)}, u32[]{:S(2)}, u32[]{:S(2)}) collective-permute-start(f32[32,64,128]{2,1,0:T(8,128)S(1)} %get-tuple-element.22), channel_id=1, source_target_pairs={{0,2},{2,0},{4,6},{6,4},{8,10},{10,8},{12,14},{14,12},{16,18},{18,... | collective-permute-start | bytes 3145736 | tf_op jit(solution)/shard_map/ppermute | solution.py:14
  30.8 26.6 %collective-permute-start.1 = (f32[32,64,128]{2,1,0:T(8,128)}, f32[32,64,128]{2,1,0:T(8,128)S(1)}, u32[]{:S(2)}, u32[]{:S(2)}) collective-permute-start(f32[32,64,128]{2,1,0:T(8,128)} %get-tuple-element.18), channel_id=1, source_target_pairs={{0,4},{4,0},{2,6},{6,2},{8,12},{12,8},{10,14},{14,10},{16,20},{20,... | collective-permute-start | bytes 3145736 | tf_op jit(solution)/shard_map/ppermute | solution.py:14
  34.2 24.5 %copy-start.5 = (bf16[1,1,1,64,64,256]{5,4,3,2,1,0:T(8,128)(2,1)S(1)}, bf16[1,1,1,64,64,256]{5,4,3,2,1,0:T(8,128)(2,1)}, u32[]{:S(2)}) copy-start(bf16[1,1,1,64,64,256]{5,4,3,2,1,0:T(8,128)(2,1)} %get-tuple-element.6) | copy-start | bytes 6291460
  34.2 24.5 %copy-start.6 = (f32[32,64,128]{2,1,0:T(8,128)S(1)}, f32[32,64,128]{2,1,0:T(8,128)}, u32[]{:S(2)}) copy-start(f32[32,64,128]{2,1,0:T(8,128)} %get-tuple-element.17) | copy-start | bytes 3145732
  65.7 24.9 %collective-permute-start.2 = (f32[32,64,128]{2,1,0:T(8,128)}, f32[32,64,128]{2,1,0:T(8,128)S(1)}, u32[]{:S(2)}, u32[]{:S(2)}) collective-permute-start(f32[32,64,128]{2,1,0:T(8,128)} %get-tuple-element.14), channel_id=1, source_target_pairs={{0,8},{8,0},{2,10},{10,2},{4,12},{12,4},{6,14},{14,6},{16,24},{24,... | collective-permute-start | bytes 3145736 | tf_op jit(solution)/shard_map/ppermute | solution.py:14
  68.0 24.0 %copy-start.4 = (bf16[1,1,1,64,64,256]{5,4,3,2,1,0:T(8,128)(2,1)S(1)}, bf16[1,1,1,64,64,256]{5,4,3,2,1,0:T(8,128)(2,1)}, u32[]{:S(2)}) copy-start(bf16[1,1,1,64,64,256]{5,4,3,2,1,0:T(8,128)(2,1)} %get-tuple-element.8) | copy-start | bytes 6291460
  68.0 24.0 %copy-start.7 = (f32[32,64,128]{2,1,0:T(8,128)S(1)}, f32[32,64,128]{2,1,0:T(8,128)}, u32[]{:S(2)}) copy-start(f32[32,64,128]{2,1,0:T(8,128)} %get-tuple-element.13) | copy-start | bytes 3145732
  97.6 47.2 %collective-permute-start.3 = (f32[32,64,128]{2,1,0:T(8,128)S(1)}, f32[32,64,128]{2,1,0:T(8,128)S(1)}, u32[]{:S(2)}, u32[]{:S(2)}) collective-permute-start(f32[32,64,128]{2,1,0:T(8,128)S(1)} %get-tuple-element.10), channel_id=1, source_target_pairs={{0,16},{16,0},{2,18},{18,2},{4,20},{20,4},{6,22},{22,6},{8,24},{24... | collective-permute-start | bytes 3145736 | tf_op jit(solution)/shard_map/ppermute | solution.py:14
  100.7 45.5 %copy-start.3 = (bf16[1,1,1,64,64,256]{5,4,3,2,1,0:T(8,128)(2,1)S(1)}, bf16[1,1,1,64,64,256]{5,4,3,2,1,0:T(8,128)(2,1)}, u32[]{:S(2)}) copy-start(bf16[1,1,1,64,64,256]{5,4,3,2,1,0:T(8,128)(2,1)} %get-tuple-element.7) | copy-start | bytes 6291460
  185.2 2.1 %copy-start.2 = (f32[32,64,128]{2,1,0:T(8,128)S(1)}, f32[32,64,128]{2,1,0:T(8,128)}, u32[]{:S(2)}) copy-start(f32[32,64,128]{2,1,0:T(8,128)} %reduce-scatter.2.cloned.1.call-done) | copy-start | bytes 3145732
  185.2 2.5 %copy-start.8 = (bf16[1,64,128,128]{3,2,1,0:T(8,128)(2,1)S(1)}, bf16[1,64,128,128]{3,2,1,0:T(8,128)(2,1)}, u32[]{:S(2)}) copy-start(bf16[1,64,128,128]{3,2,1,0:T(8,128)(2,1)} %param.9) | copy-start | bytes 6291460
  187.3 2.8 %copy-start.1 = (bf16[64,64,256]{2,1,0:T(8,128)(2,1)S(1)}, bf16[64,64,256]{2,1,0:T(8,128)(2,1)}, u32[]{:S(2)}) copy-start(bf16[64,64,256]{2,1,0:T(8,128)(2,1)} %param.6) | copy-start | bytes 6291460
Sparse Core Ops, SparseCore 0:
  152.6 32.5 reduce-scatter.1
where the time goes:
time: 197 us
  waiting for transfers between devices  123 us (62%)
  matrix products  24.3 us (12%)
  other arithmetic  19 us (10%)
  between operations  13.6 us (7%)
  local copies, waits for them, and re-layouts  9.67 us (5%)
  starting transfers between devices  7.8 us (4%)
    ppermute x4, waiting for transfers between devices, from_partner(): return lax.ppermute(block, axis, route)  89.8 us
    reduce_scatter x1, waiting for transfers between devices, shards(): total = lax.psum_scatter(coeff, 'col', scatter_dimension=0, tiled=True)  32.7 us
    dot_general x4, matrix products, mix_level(): jnp.einsum('jskm,jmn->jskn', weights, stacked, precision=lax.Precision.HI...  18.1 us
    neg x10, other arithmetic, complex_stack(): flipped = jnp.concatenate([-block[..., middle:], block[..., :middle]], -1)  14.3 us
    ppermute x4, starting transfers between devices, from_partner(): return lax.ppermute(block, axis, route)  7.8 us
    slice x1, local copies, waits for them, and re-layouts, shards(): transfer[level, 0, 0]  5.65 us
    select_n x4, other arithmetic, mix_level(): return jnp.where(live_rows[..., None], mixed, jnp.float32(0.0))  4.47 us
  transfers between devices with their start and end apart: 5, of which 4 were waited for; matrix products, arithmetic and copies ran while one was open for 4% of the time, Pallas kernels for 0%

commit v1 on v0

v1 whole, which is shorter than its diff:
```python
import functools

import jax
import jax.numpy as jnp
from jax import lax
from jax.experimental import pallas as pl
from jax.experimental.pallas import tpu as pltpu
from jax.sharding import PartitionSpec as P

MESH = pl.DeviceIdType.MESH
F32 = jnp.float32
BF16 = jnp.bfloat16


def rotated(z):
    middle = z.shape[1] // 2
    lane = lax.broadcasted_iota(jnp.int32, z.shape, 1)
    turned = pltpu.roll(z, middle, 1)
    return jnp.where(lane < middle, -turned, turned)


def split_dot(matrix, stacked):
    high = stacked.astype(BF16)
    low = (stacked - high.astype(F32)).astype(BF16)
    both = jnp.dot(matrix, jnp.concatenate([high, low], 1), preferred_element_type=F32)
    columns = stacked.shape[1]
    return both[:, :columns] + both[:, columns:]


def kernel(
    sizes, ranks, rhs_hbm, leaf_hbm, transfer_hbm, basis_hbm, result_hbm,
    rhs, leaf, transfer, basis, result, coeff, arrived, shared,
    load_sem, out_sem, send_sem, recv_sem, share_send, share_recv,
):
    levels, chunks, owned, n_col, points, rank_cap = sizes
    block_count = 1 << levels
    half = block_count // 2
    quarter = half // 2
    p = lax.axis_index("row")
    c = lax.axis_index("col")
    bits = [(p // (1 << level)) % 2 for level in range(levels)] + [1]
    partners = [p + (1 - 2 * bits[level]) * (1 << level) for level in range(levels)]
    piece = min(block_count, owned)
    own_chunks = max(1, chunks // n_col)
    first = (c * chunks) // n_col + own_chunks
    order = [(first + n) % chunks for n in range(chunks)]

    loads = {}

    def load(name, source, target):
        copy = pltpu.make_async_copy(source, target, load_sem.at[len(loads)])
        copy.start()
        loads[name] = copy

    for n in range(chunks):
        load(("rhs", n), rhs_hbm.at[:, order[n]], rhs.at[n])
        load(("leaf", n), leaf_hbm.at[:, order[n]], leaf.at[n])
        if n == 0:
            load(("transfer", 0), transfer_hbm.at[0], transfer.at[0])
    for level in range(1, levels):
        load(("transfer", level), transfer_hbm.at[level], transfer.at[level])
    load("basis", basis_hbm.at[pl.ds(c * owned, owned)], basis)

    barrier = pltpu.get_barrier_semaphore()
    for level in range(levels):
        pl.semaphore_signal(barrier, 1, device_id={"row": partners[level]}, device_id_type=MESH)
    for step in range(1, n_col):
        pl.semaphore_signal(barrier, 1, device_id={"col": (c + step) % n_col}, device_id_type=MESH)
    pl.semaphore_wait(barrier, levels + n_col - 1)

    waited = set()

    def loaded(name):
        if name not in waited:
            waited.add(name)
            loads[name].wait()

    def part(level, h):
        if level == levels - 1:
            return h
        return 1 - bits[level + 1] if h == 0 else bits[level + 1]

    def exchange(level, n, h):
        at = part(level, h) * quarter
        return pltpu.make_async_remote_copy(
            src_ref=coeff.at[level, n, pl.ds((1 - bits[level]) * half + at, quarter)],
            dst_ref=arrived.at[level, n, pl.ds(at, quarter)],
            send_sem=send_sem.at[level, n, h],
            recv_sem=recv_sem.at[level, n, h],
            device_id={"row": partners[level]},
            device_id_type=MESH,
        )

    def leaf_block(n, f):
        z = rhs[n, f].astype(F32)
        stacked = jnp.concatenate([z, rotated(z)], 0).astype(BF16)
        coeff[0, n, f] = jnp.dot(leaf[n, f], stacked, preferred_element_type=F32)

    def leaf_blocks(n, start, count):
        def body(i, carry):
            leaf_block(n, start + 2 * i)
            leaf_block(n, start + 2 * i + 1)
            return carry

        lax.fori_loop(0, count // 2, body, 0)

    def mix_block(level, n, m):
        low = m % (1 << level)
        high = m // (1 << level)
        j = high * (chunks << level) + order[n] * (1 << level) + low
        own = coeff[level, n, bits[level] * half + m]
        other = arrived[level, n, m]
        stacked = jnp.concatenate([own, rotated(own), other, rotated(other)], 0)
        mixed = split_dot(transfer[level, j], stacked)
        row = lax.broadcasted_iota(jnp.int32, (rank_cap, mixed.shape[1]), 0)
        for s in range(2):
            live = row < ranks[level, 2 * j + s]
            coeff[level + 1, n, 2 * m + s] = jnp.where(
                live, mixed[s * rank_cap : (s + 1) * rank_cap], 0.0
            )

    def mix_blocks(level, n, start, count):
        def body(i, carry):
            mix_block(level, n, start + 2 * i)
            mix_block(level, n, start + 2 * i + 1)
            return carry

        if count == 2:
            body(0, 0)
        else:
            lax.fori_loop(0, count // 2, body, 0)

    def leaves_of(n):
        loaded(("rhs", n))
        loaded(("leaf", n))
        sent = (1 - bits[0]) * half
        for h in range(2):
            leaf_blocks(n, sent + part(0, h) * quarter, quarter)
            exchange(0, n, h).start()
        leaf_blocks(n, bits[0] * half, half)

    def mix(level, n):
        loaded(("transfer", level))
        for h in range(2):
            exchange(level, n, h).wait_recv()
            start = part(level, h) * quarter
            if h == 0 and level + 1 < levels:
                for k in range(2):
                    mix_blocks(level, n, start + part(level + 1, k) * (quarter // 2), quarter // 2)
                    exchange(level + 1, n, k).start()
            else:
                mix_blocks(level, n, start, quarter)

    def share(n, k):
        g = order[n] * block_count + k * piece
        owner = g // owned
        slot = (g % owned) // piece
        return owner, pltpu.make_async_remote_copy(
            src_ref=coeff.at[levels, n, pl.ds(k * piece, piece)],
            dst_ref=shared.at[c, pl.ds(slot * piece, piece)],
            send_sem=share_send.at[n, k],
            recv_sem=share_recv.at[c, slot],
            device_id={"col": owner},
            device_id_type=MESH,
        )

    pieces = block_count // piece

    def each_share(act):
        for n in range(chunks):
            act_on_share(n, act)

    def act_on_share(n, act):
        if chunks >= n_col:
            if n < chunks - own_chunks:
                act(share(n, 0)[1])
            return
        for k in range(pieces):
            owner, copy = share(n, k)

            @pl.when(owner != c)
            def _():
                act(copy)

    def share_out(n):
        act_on_share(n, lambda copy: copy.start())

    def receive_shares(slot):
        for step in range(1, n_col):
            sender = (c + step) % n_col
            pltpu.make_async_remote_copy(
                src_ref=coeff.at[levels, 0, pl.ds(0, piece)],
                dst_ref=shared.at[sender, pl.ds(slot * piece, piece)],
                send_sem=share_send.at[0, 0],
                recv_sem=share_recv.at[sender, slot],
                device_id={"col": sender},
                device_id_type=MESH,
            ).wait_recv()

    def target_block(n, f, g):
        total = coeff[levels, n, f]
        for step in range(1, n_col):
            total = total + shared[(c + step) % n_col, g]
        stacked = jnp.concatenate([total, rotated(total)], 0)
        result[g] = split_dot(basis[g], stacked).astype(BF16)

    def targets_of(n):
        loaded("basis")
        slot = n - (chunks - own_chunks)
        receive_shares(slot)
        begin = 0
        if chunks < n_col:
            begin = (c * owned) % block_count

        def body(i, carry):
            for u in range(2):
                f = 2 * i + u
                target_block(n, begin + f, slot * piece + f)
            return carry

        lax.fori_loop(0, piece // 2, body, 0)
        copy = pltpu.make_async_copy(
            result.at[pl.ds(slot * piece, piece)],
            result_hbm.at[pl.ds(slot * piece, piece)],
            out_sem.at[slot],
        )
        copy.start()
        return copy

    finals = []

    def run(stage, n):
        if stage == 0:
            leaves_of(n)
            return
        mix(stage - 1, n)
        if stage == levels:
            share_out(n)
            if n >= chunks - own_chunks:
                finals.append(targets_of(n))

    plan = []
    placed = set()

    def place(stage, n):
        if 0 <= n < chunks and 0 <= stage <= levels and (stage, n) not in placed:
            placed.add((stage, n))
            plan.append((stage, n))

    for stage, n in (
        (0, 0), (0, 1), (1, 0), (0, 2), (1, 1), (2, 0), (1, 2), (0, 3), (3, 0),
        (1, 3), (2, 1), (3, 1), (2, 2), (2, 3), (3, 2), (3, 3),
    ):
        place(stage, n)
    for stage in range(levels + 1):
        for n in range(chunks):
            place(stage, n)
    for stage, n in plan:
        run(stage, n)

    for level in range(levels):
        for n in range(chunks):
            for h in range(2):
                exchange(level, n, h).wait_send()
    each_share(lambda copy: copy.wait_send())
    for copy in finals:
        copy.wait()


def shards(rhs, leaf_basis, transfer, ranks, out_basis):
    leaves, rank_cap, width = leaf_basis.shape
    points = width // 2
    columns = rhs.shape[1]
    levels = transfer.shape[0]
    n_col = lax.axis_size("col")
    owned = leaves // n_col
    block_count = 1 << levels
    half = block_count // 2
    chunks = leaves // block_count
    piece = min(block_count, owned)
    sizes = (levels, chunks, owned, n_col, points, rank_cap)
    any_space = pl.BlockSpec(memory_space=pl.ANY)
    result = pl.pallas_call(
        functools.partial(kernel, sizes),
        out_shape=jax.ShapeDtypeStruct((owned, points, columns), BF16),
        in_specs=[pl.BlockSpec(memory_space=pltpu.SMEM)] + [any_space] * 4,
        out_specs=any_space,
        scratch_shapes=[
            pltpu.VMEM((chunks, block_count, points, columns), BF16),
            pltpu.VMEM((chunks, block_count, rank_cap, width), BF16),
            pltpu.VMEM((levels, leaves // 2, 2 * rank_cap, 4 * rank_cap), BF16),
            pltpu.VMEM((owned, points, 2 * rank_cap), BF16),
            pltpu.VMEM((owned, points, columns), BF16),
            pltpu.VMEM((levels + 1, chunks, block_count, rank_cap, columns), F32),
            pltpu.VMEM((levels, chunks, half, rank_cap, columns), F32),
            pltpu.VMEM((n_col, owned, rank_cap, columns), F32),
            pltpu.SemaphoreType.DMA((2 * chunks + levels + 1,)),
            pltpu.SemaphoreType.DMA((owned // piece,)),
            pltpu.SemaphoreType.DMA((levels, chunks, 2)),
            pltpu.SemaphoreType.DMA((levels, chunks, 2)),
            pltpu.SemaphoreType.DMA((chunks, block_count // piece)),
            pltpu.SemaphoreType.DMA((n_col, owned // piece)),
        ],
        compiler_params=pltpu.CompilerParams(
            collective_id=0, has_side_effects=True, vmem_limit_bytes=48 * 1024 * 1024
        ),
    )(
        ranks.reshape(levels, leaves),
        rhs.reshape(block_count, chunks, points, columns),
        leaf_basis.reshape(block_count, chunks, rank_cap, width),
        transfer.reshape(levels, leaves // 2, 2 * rank_cap, 4 * rank_cap),
        out_basis.reshape(leaves, points, 2 * rank_cap),
    )
    return result.reshape(owned * points, columns)


def solution(mesh):
    in_specs = (
        P(("row", "col"), None),
        P(("row", "col"), None, None),
        P(None, "row", "col", None, None, None),
        P(None, "row", "col", None),
        P("row", None, None, None),
    )
    out_specs = P(("row", "col"), None)
    return jax.shard_map(shards, mesh=mesh, in_specs=in_specs, out_specs=out_specs, check_vma=False)
```

time: 197 us -> 96 us (0.49)
  waiting for transfers between devices: 123 us -> 0 us
  Pallas kernels: 0 us -> 91 us
  matrix products: 24.3 us -> 0 us
  other arithmetic: 19 us -> 0 us
  between operations: 13.6 us -> 0.01 us
  starting transfers between devices: 7.8 us -> 0 us
  local copies, waits for them, and re-layouts: 9.67 us -> 4.83 us
    pallas_call x0 -> x1, Pallas kernels: none -> 91 us  [shards(): pl.pallas_call(functools.partial(kernel, sizes), out_shape=jax.ShapeDtype...]
    ppermute x4 -> x0, waiting for transfers between devices: 89.8 us -> none  [from_partner(): return lax.ppermute(block, axis, route)]
    reduce_scatter x1 -> x0, waiting for transfers between devices: 32.7 us -> none  [shards(): total = lax.psum_scatter(coeff, 'col', scatter_dimension=0, tiled=True)]
    dot_general x6 -> x0, matrix products: 24.3 us -> none  [the longest x4 18.1 us: mix_level(): jnp.einsum('jskm,jmn->jskn', weights, stacked, precision=lax.Precision.HI...]
    neg x10 -> x0, other arithmetic: 14.3 us -> none  [complex_stack(): flipped = jnp.concatenate([-block[..., middle:], block[..., :middle]], -1)]
    ppermute x4 -> x0, starting transfers between devices: 7.8 us -> none  [from_partner(): return lax.ppermute(block, axis, route)]
    slice x1 -> x0, local copies, waits for them, and re-layouts: 5.65 us -> none  [shards(): transfer[level, 0, 0]]
    select_n x4 -> x0, other arithmetic: 4.47 us -> none  [mix_level(): return jnp.where(live_rows[..., None], mixed, jnp.float32(0.0))]
  transfers between devices with their start and end apart: 5 -> 0, of which waited for: 4 -> 0; matrix products, arithmetic and copies ran while one was open for 4% -> 0% of each run, Pallas kernels for 0% -> 0%
where the time goes in v1:
time: 96 us; the launch traced here: 95.8 us
  Pallas kernels  91 us (95%)
  local copies, waits for them, and re-layouts  4.83 us (5%)
    pallas_call x1, Pallas kernels, shards(): pl.pallas_call(functools.partial(kernel, sizes), out_shape=jax.ShapeDtype...  91 us
    unnamed x7, local copies, waits for them, and re-layouts  4.83 us

profile of v1, /device:TPU:0, one launch (start us, length us, event | category | flops | bytes accessed | tf_op | source)
XLA Modules:
  0.0 95.8 jit_solution(7512774511018162543)
XLA Ops:
  0.0 0.0 copy-start
  0.0 1.6 %copy-done = bf16[8192,128]{1,0:T(8,128)(2,1)S(1)} copy-done((bf16[8192,128]{1,0:T(8,128)(2,1)S(1)}, bf16[8192,128]{1,0:T(8,128)(2,1)}, u32[]{:S(2)}) %copy-start) | copy-done | bytes 2097176
  1.6 0.0 copy-start.1
  1.6 1.6 %copy-done.1 = bf16[64,64,256]{2,1,0:T(8,128)(2,1)S(1)} copy-done((bf16[64,64,256]{2,1,0:T(8,128)(2,1)S(1)}, bf16[64,64,256]{2,1,0:T(8,128)(2,1)}, u32[]{:S(2)}) %copy-start.1) | copy-done | bytes 2097176
  3.2 0.0 copy-start.2
  3.2 0.7 copy-done.2
  3.9 91.0 %shard_map.55 = bf16[32,128,128]{2,1,0:T(8,128)(2,1)S(1)} custom-call(s32[4,64]{1,0:T(4,128)S(1)} %bitcast.9, bf16[16,4,128,128]{3,2,1,0:T(8,128)(2,1)S(1)} %bitcast.7, bf16[16,4,64,256]{3,2,1,0:T(8,128)(2,1)S(1)} %bitcast.8, bf16[4,32,128,256]{3,2,1,0:T(8,128)(2,1)} %bitcast.10, bf16[64,128,128]{2,1,0:T(8,128)(2,1)} %bitcast.11), custom_call_target="tpu_custom_call" | custom-call | tf_op jit(solution)/shard_map/pallas_call | solution.py:283
  94.8 1.0 %copy.7 = bf16[4096,128]{1,0:T(8,128)(2,1)} copy(bf16[4096,128]{1,0:T(8,128)(2,1)S(1)} %bitcast.6) | data formatting | bytes 2097152
Async XLA Ops:
  0.0 1.6 %copy-start = (bf16[8192,128]{1,0:T(8,128)(2,1)S(1)}, bf16[8192,128]{1,0:T(8,128)(2,1)}, u32[]{:S(2)}) copy-start(bf16[8192,128]{1,0:T(8,128)(2,1)} %param.5) | copy-start | bytes 6291460
  1.6 1.6 %copy-start.1 = (bf16[64,64,256]{2,1,0:T(8,128)(2,1)S(1)}, bf16[64,64,256]{2,1,0:T(8,128)(2,1)}, u32[]{:S(2)}) copy-start(bf16[64,64,256]{2,1,0:T(8,128)(2,1)} %param.6) | copy-start | bytes 6291460
  3.2 0.7 copy-start.2

commit v2 on v1

--- a/solution.py
+++ b/solution.py
@@ -10,6 +10,15 @@
 MESH = pl.DeviceIdType.MESH
 F32 = jnp.float32
 BF16 = jnp.bfloat16
+PLAN = (
+    (0, 0, 0), (0, 0, 1), (0, 1, 0), (1, 0, 0), (1, 0, 1), (0, 1, 1),
+    (1, 1, 0), (1, 1, 1), (2, 0, 0), (0, 2, 0), (0, 2, 1), (2, 0, 1),
+    (1, 2, 0), (3, 0, 0), (2, 1, 0), (1, 2, 1), (3, 0, 1), (2, 1, 1),
+    (0, 3, 0), (2, 2, 0), (0, 3, 1), (1, 3, 0), (2, 2, 1), (1, 3, 1),
+    (4, 0, 0), (2, 3, 0), (3, 1, 0), (4, 0, 1), (2, 3, 1), (3, 1, 1),
+    (3, 2, 0), (4, 1, 0), (3, 2, 1), (3, 3, 0), (4, 1, 1), (3, 3, 1),
+    (4, 2, 0), (4, 2, 1), (5, 2, 0), (4, 3, 0), (4, 3, 1), (5, 3, 0),
+)
 
 
 def rotated(z):
@@ -91,18 +100,29 @@
             device_id_type=MESH,
         )
 
+    def in_loop(count, act):
+        width = min(4, count)
+
+        def body(i, carry):
+            stores = [act(width * i + u) for u in range(width)]
+            for ref, rows in stores:
+                for at, block in rows:
+                    ref[at] = block
+            return carry
+
+        if count == width:
+            body(0, 0)
+        else:
+            lax.fori_loop(0, count // width, body, 0)
+
     def leaf_block(n, f):
-        z = rhs[n, f].astype(F32)
-        stacked = jnp.concatenate([z, rotated(z)], 0).astype(BF16)
-        coeff[0, n, f] = jnp.dot(leaf[n, f], stacked, preferred_element_type=F32)
+        matrix = leaf[n, f]
+        parts = jnp.concatenate([matrix[:, :points], matrix[:, points:]], 0)
+        both = jnp.dot(parts, rhs[n, f], preferred_element_type=F32)
+        return coeff, [((0, n, f), both[:rank_cap] + rotated(both[rank_cap:]))]
 
     def leaf_blocks(n, start, count):
-        def body(i, carry):
-            leaf_block(n, start + 2 * i)
-            leaf_block(n, start + 2 * i + 1)
-            return carry
-
-        lax.fori_loop(0, count // 2, body, 0)
+        in_loop(count, lambda i: leaf_block(n, start + i))
 
     def mix_block(level, n, m):
         low = m % (1 << level)
@@ -113,43 +133,37 @@
         stacked = jnp.concatenate([own, rotated(own), other, rotated(other)], 0)
         mixed = split_dot(transfer[level, j], stacked)
         row = lax.broadcasted_iota(jnp.int32, (rank_cap, mixed.shape[1]), 0)
+        rows = []
         for s in range(2):
             live = row < ranks[level, 2 * j + s]
-            coeff[level + 1, n, 2 * m + s] = jnp.where(
-                live, mixed[s * rank_cap : (s + 1) * rank_cap], 0.0
-            )
+            block = jnp.where(live, mixed[s * rank_cap : (s + 1) * rank_cap], 0.0)
+            rows.append(((level + 1, n, 2 * m + s), block))
+        return coeff, rows
 
     def mix_blocks(level, n, start, count):
-        def body(i, carry):
-            mix_block(level, n, start + 2 * i)
-            mix_block(level, n, start + 2 * i + 1)
-            return carry
-
-        if count == 2:
-            body(0, 0)
-        else:
-            lax.fori_loop(0, count // 2, body, 0)
-
-    def leaves_of(n):
+        in_loop(count, lambda i: mix_block(level, n, start + i))
+
+    def leaves_of(n, h):
         loaded(("rhs", n))
         loaded(("leaf", n))
+        if h == 1:
+            leaf_blocks(n, bits[0] * half, half)
+            return
         sent = (1 - bits[0]) * half
-        for h in range(2):
-            leaf_blocks(n, sent + part(0, h) * quarter, quarter)
-            exchange(0, n, h).start()
-        leaf_blocks(n, bits[0] * half, half)
-
-    def mix(level, n):
+        for k in range(2):
+            leaf_blocks(n, sent + part(0, k) * quarter, quarter)
+            exchange(0, n, k).start()
+
+    def mix(level, n, h):
         loaded(("transfer", level))
-        for h in range(2):
-            exchange(level, n, h).wait_recv()
-            start = part(level, h) * quarter
-            if h == 0 and level + 1 < levels:
-                for k in range(2):
-                    mix_blocks(level, n, start + part(level + 1, k) * (quarter // 2), quarter // 2)
-                    exchange(level + 1, n, k).start()
-            else:
-                mix_blocks(level, n, start, quarter)
+        exchange(level, n, h).wait_recv()
+        start = part(level, h) * quarter
+        if h == 1 or level + 1 == levels:
+            mix_blocks(level, n, start, quarter)
+            return
+        for k in range(2):
+            mix_blocks(level, n, start + part(level + 1, k) * (quarter // 2), quarter // 2)
+            exchange(level + 1, n, k).start()
 
     def share(n, k):
         g = order[n] * block_count + k * piece
@@ -202,7 +216,7 @@
         for step in range(1, n_col):
             total = total + shared[(c + step) % n_col, g]
         stacked = jnp.concatenate([total, rotated(total)], 0)
-        result[g] = split_dot(basis[g], stacked).astype(BF16)
+        return result, [(g, split_dot(basis[g], stacked).astype(BF16))]
 
     def targets_of(n):
         loaded("basis")
@@ -212,13 +226,7 @@
         if chunks < n_col:
             begin = (c * owned) % block_count
 
-        def body(i, carry):
-            for u in range(2):
-                f = 2 * i + u
-                target_block(n, begin + f, slot * piece + f)
-            return carry
-
-        lax.fori_loop(0, piece // 2, body, 0)
+        in_loop(piece, lambda i: target_block(n, begin + i, slot * piece + i))
         copy = pltpu.make_async_copy(
             result.at[pl.ds(slot * piece, piece)],
             result_hbm.at[pl.ds(slot * piece, piece)],
@@ -229,34 +237,24 @@
 
     finals = []
 
-    def run(stage, n):
+    def run(stage, n, h):
         if stage == 0:
-            leaves_of(n)
-            return
-        mix(stage - 1, n)
-        if stage == levels:
-            share_out(n)
-            if n >= chunks - own_chunks:
-                finals.append(targets_of(n))
-
-    plan = []
-    placed = set()
-
-    def place(stage, n):
-        if 0 <= n < chunks and 0 <= stage <= levels and (stage, n) not in placed:
-            placed.add((stage, n))
-            plan.append((stage, n))
-
-    for stage, n in (
-        (0, 0), (0, 1), (1, 0), (0, 2), (1, 1), (2, 0), (1, 2), (0, 3), (3, 0),
-        (1, 3), (2, 1), (3, 1), (2, 2), (2, 3), (3, 2), (3, 3),
-    ):
-        place(stage, n)
-    for stage in range(levels + 1):
+            leaves_of(n, h)
+        elif stage <= levels:
+            mix(stage - 1, n, h)
+            if stage == levels and h == 1:
+                share_out(n)
+        elif n >= chunks - own_chunks:
+            finals.append(targets_of(n))
+
+    plan = list(PLAN) if (levels, chunks) == (4, 4) else []
+    for stage in range(levels + 2):
         for n in range(chunks):
-            place(stage, n)
-    for stage, n in plan:
-        run(stage, n)
+            for h in range(1 if stage > levels else 2):
+                if (stage, n, h) not in plan:
+                    plan.append((stage, n, h))
+    for stage, n, h in plan:
+        run(stage, n, h)
 
     for level in range(levels):
         for n in range(chunks):
@@ -302,7 +300,7 @@
             pltpu.SemaphoreType.DMA((n_col, owned // piece)),
         ],
         compiler_params=pltpu.CompilerParams(
-            collective_id=0, has_side_effects=True, vmem_limit_bytes=48 * 1024 * 1024
+            collective_id=0, has_side_effects=True, vmem_limit_bytes=56 * 1024 * 1024
         ),
     )(
         ranks.reshape(levels, leaves),

time: 96 us -> 71.2 us (0.74)
  Pallas kernels: 91 us -> 68.7 us
  local copies, waits for them, and re-layouts: 4.83 us -> 2.26 us
    pallas_call x1, Pallas kernels: 91 us -> 68.7 us  [shards(): pl.pallas_call(functools.partial(kernel, sizes), out_shape=jax.ShapeDtype...]
    unnamed x7 -> x1, local copies, waits for them, and re-layouts: 4.83 us -> 2.26 us
where the time goes in v2:
time: 71.2 us; the launch traced here: 71 us
  Pallas kernels  68.7 us (96%)
  local copies, waits for them, and re-layouts  2.26 us (3%)
    pallas_call x1, Pallas kernels, shards(): pl.pallas_call(functools.partial(kernel, sizes), out_shape=jax.ShapeDtype...  68.7 us
    unnamed x1, local copies, waits for them, and re-layouts  2.26 us

profile of v2, /device:TPU:0, one launch (start us, length us, event | category | flops | bytes accessed | tf_op | source)
XLA Modules:
  0.0 71.0 jit_solution(12226918265268316286)
XLA Ops:
  0.0 68.7 %shard_map.55 = bf16[32,128,128]{2,1,0:T(8,128)(2,1)} custom-call(s32[4,64]{1,0:T(4,128)} %bitcast.11, bf16[16,4,128,128]{3,2,1,0:T(8,128)(2,1)} %bitcast.8, bf16[16,4,64,256]{3,2,1,0:T(8,128)(2,1)} %bitcast.9, bf16[4,32,128,256]{3,2,1,0:T(8,128)(2,1)} %bitcast.6, bf16[64,128,128]{2,1,0:T(8,128)(2,1)} %bitcast.10), custom_call_target="tpu_custom_call" | custom-call | tf_op jit(solution)/shard_map/pallas_call | solution.py:281
  68.7 2.3 %copy.7 = bf16[4096,128]{1,0:T(8,128)(2,1)} copy(bf16[4096,128]{1,0:T(8,128)(2,1)} %bitcast.7) | data formatting | bytes 2097152

commit v3 on v2

--- a/solution.py
+++ b/solution.py
@@ -12,12 +12,13 @@
 BF16 = jnp.bfloat16
 PLAN = (
     (0, 0, 0), (0, 0, 1), (0, 1, 0), (1, 0, 0), (1, 0, 1), (0, 1, 1),
-    (1, 1, 0), (1, 1, 1), (2, 0, 0), (0, 2, 0), (0, 2, 1), (2, 0, 1),
-    (1, 2, 0), (3, 0, 0), (2, 1, 0), (1, 2, 1), (3, 0, 1), (2, 1, 1),
-    (0, 3, 0), (2, 2, 0), (0, 3, 1), (1, 3, 0), (2, 2, 1), (1, 3, 1),
-    (4, 0, 0), (2, 3, 0), (3, 1, 0), (4, 0, 1), (2, 3, 1), (3, 1, 1),
-    (3, 2, 0), (4, 1, 0), (3, 2, 1), (3, 3, 0), (4, 1, 1), (3, 3, 1),
-    (4, 2, 0), (4, 2, 1), (5, 2, 0), (4, 3, 0), (4, 3, 1), (5, 3, 0),
+    (1, 1, 0), (1, 1, 1), (0, 2, 0), (2, 0, 0), (0, 2, 1), (1, 2, 0),
+    (2, 0, 1), (1, 2, 1), (0, 3, 0), (3, 0, 0), (2, 1, 0), (0, 3, 1),
+    (1, 3, 0), (1, 3, 1), (2, 1, 1), (2, 2, 0), (2, 2, 1), (2, 3, 0),
+    (3, 0, 1), (4, 0, 0), (4, 0, 1), (2, 3, 1), (3, 1, 0), (3, 2, 0),
+    (3, 3, 0), (3, 1, 1), (4, 1, 0), (4, 1, 1), (3, 2, 1), (4, 2, 0),
+    (4, 2, 1), (5, 2, 0), (5, 2, 1), (3, 3, 1), (4, 3, 0), (4, 3, 1),
+    (5, 3, 0), (5, 3, 1),
 )
 
 
@@ -90,15 +91,26 @@
         return 1 - bits[level + 1] if h == 0 else bits[level + 1]
 
     def exchange(level, n, h):
-        at = part(level, h) * quarter
-        return pltpu.make_async_remote_copy(
-            src_ref=coeff.at[level, n, pl.ds((1 - bits[level]) * half + at, quarter)],
-            dst_ref=arrived.at[level, n, pl.ds(at, quarter)],
-            send_sem=send_sem.at[level, n, h],
-            recv_sem=recv_sem.at[level, n, h],
-            device_id={"row": partners[level]},
-            device_id_type=MESH,
-        )
+        count = 2 if n == 0 and 0 < level < levels - 1 else 1
+        size = quarter // count
+        copies = []
+        for k in range(count):
+            at = part(level, h) * quarter + (part(level + 1, k) * size if count == 2 else 0)
+            copies.append(
+                pltpu.make_async_remote_copy(
+                    src_ref=coeff.at[level, n, pl.ds((1 - bits[level]) * half + at, size)],
+                    dst_ref=arrived.at[level, n, pl.ds(at, size)],
+                    send_sem=send_sem.at[level, n, h, k],
+                    recv_sem=recv_sem.at[level, n, h, k],
+                    device_id={"row": partners[level]},
+                    device_id_type=MESH,
+                )
+            )
+        return copies
+
+    def send(level, n, h):
+        for copy in exchange(level, n, h):
+            copy.start()
 
     def in_loop(count, act):
         width = min(4, count)
@@ -152,18 +164,25 @@
         sent = (1 - bits[0]) * half
         for k in range(2):
             leaf_blocks(n, sent + part(0, k) * quarter, quarter)
-            exchange(0, n, k).start()
+            send(0, n, k)
 
     def mix(level, n, h):
         loaded(("transfer", level))
-        exchange(level, n, h).wait_recv()
+        copies = exchange(level, n, h)
         start = part(level, h) * quarter
         if h == 1 or level + 1 == levels:
+            for copy in copies:
+                copy.wait_recv()
             mix_blocks(level, n, start, quarter)
             return
         for k in range(2):
+            if k < len(copies):
+                copies[k].wait_recv()
             mix_blocks(level, n, start + part(level + 1, k) * (quarter // 2), quarter // 2)
-            exchange(level + 1, n, k).start()
+            if k == 0 or level + 1 != levels - 2:
+                send(level + 1, n, k)
+        if level == levels - 2:
+            send(level, n, 1)
 
     def share(n, k):
         g = order[n] * block_count + k * piece
@@ -218,22 +237,23 @@
         stacked = jnp.concatenate([total, rotated(total)], 0)
         return result, [(g, split_dot(basis[g], stacked).astype(BF16))]
 
-    def targets_of(n):
-        loaded("basis")
+    def targets_of(n, h):
         slot = n - (chunks - own_chunks)
-        receive_shares(slot)
-        begin = 0
-        if chunks < n_col:
-            begin = (c * owned) % block_count
-
-        in_loop(piece, lambda i: target_block(n, begin + i, slot * piece + i))
+        begin, count = h * half, half
+        if piece < block_count:
+            if h == 0:
+                return
+            begin, count = (c * owned) % block_count, piece
+        if h == 0 or piece < block_count:
+            loaded("basis")
+            receive_shares(slot)
+        g = slot * piece + (h * half if piece == block_count else 0)
+        in_loop(count, lambda i: target_block(n, begin + i, g + i))
         copy = pltpu.make_async_copy(
-            result.at[pl.ds(slot * piece, piece)],
-            result_hbm.at[pl.ds(slot * piece, piece)],
-            out_sem.at[slot],
+            result.at[pl.ds(g, count)], result_hbm.at[pl.ds(g, count)], out_sem.at[slot, h]
         )
         copy.start()
-        return copy
+        finals.append(copy)
 
     finals = []
 
@@ -245,12 +265,12 @@
             if stage == levels and h == 1:
                 share_out(n)
         elif n >= chunks - own_chunks:
-            finals.append(targets_of(n))
+            targets_of(n, h)
 
     plan = list(PLAN) if (levels, chunks) == (4, 4) else []
     for stage in range(levels + 2):
         for n in range(chunks):
-            for h in range(1 if stage > levels else 2):
+            for h in range(2):
                 if (stage, n, h) not in plan:
                     plan.append((stage, n, h))
     for stage, n, h in plan:
@@ -259,7 +279,8 @@
     for level in range(levels):
         for n in range(chunks):
             for h in range(2):
-                exchange(level, n, h).wait_send()
+                for copy in exchange(level, n, h):
+                    copy.wait_send()
     each_share(lambda copy: copy.wait_send())
     for copy in finals:
         copy.wait()
@@ -293,9 +314,9 @@
             pltpu.VMEM((levels, chunks, half, rank_cap, columns), F32),
             pltpu.VMEM((n_col, owned, rank_cap, columns), F32),
             pltpu.SemaphoreType.DMA((2 * chunks + levels + 1,)),
-            pltpu.SemaphoreType.DMA((owned // piece,)),
-            pltpu.SemaphoreType.DMA((levels, chunks, 2)),
-            pltpu.SemaphoreType.DMA((levels, chunks, 2)),
+            pltpu.SemaphoreType.DMA((owned // piece, 2)),
+            pltpu.SemaphoreType.DMA((levels, chunks, 2, 2)),
+            pltpu.SemaphoreType.DMA((levels, chunks, 2, 2)),
             pltpu.SemaphoreType.DMA((chunks, block_count // piece)),
             pltpu.SemaphoreType.DMA((n_col, owned // piece)),
         ],

time: 71.2 us -> 73.9 us (1.038)
  Pallas kernels: 68.7 us -> 71.4 us
    pallas_call x1, Pallas kernels: 68.7 us -> 71.4 us  [shards(): pl.pallas_call(functools.partial(kernel, sizes), out_shape=jax.ShapeDtype...]
where the time goes in v3:
time: 73.9 us; the launch traced here: 73.7 us
  Pallas kernels  71.4 us (97%)
  local copies, waits for them, and re-layouts  2.26 us (3%)
    pallas_call x1, Pallas kernels, shards(): pl.pallas_call(functools.partial(kernel, sizes), out_shape=jax.ShapeDtype...  71.4 us
    unnamed x1, local copies, waits for them, and re-layouts  2.26 us

profile of v3, /device:TPU:0, one launch (start us, length us, event | category | flops | bytes accessed | tf_op | source)
XLA Modules:
  0.0 73.7 jit_solution(18410570627575931817)
XLA Ops:
  0.0 71.4 %shard_map.55 = bf16[32,128,128]{2,1,0:T(8,128)(2,1)} custom-call(s32[4,64]{1,0:T(4,128)} %bitcast.11, bf16[16,4,128,128]{3,2,1,0:T(8,128)(2,1)} %bitcast.8, bf16[16,4,64,256]{3,2,1,0:T(8,128)(2,1)} %bitcast.9, bf16[4,32,128,256]{3,2,1,0:T(8,128)(2,1)} %bitcast.6, bf16[64,128,128]{2,1,0:T(8,128)(2,1)} %bitcast.10), custom_call_target="tpu_custom_call" | custom-call | tf_op jit(solution)/shard_map/pallas_call | solution.py:302
  71.4 2.3 %copy.7 = bf16[4096,128]{1,0:T(8,128)(2,1)} copy(bf16[4096,128]{1,0:T(8,128)(2,1)} %bitcast.7) | data formatting | bytes 2097152

commit v4 on v3

--- a/solution.py
+++ b/solution.py
@@ -12,13 +12,13 @@
 BF16 = jnp.bfloat16
 PLAN = (
     (0, 0, 0), (0, 0, 1), (0, 1, 0), (1, 0, 0), (1, 0, 1), (0, 1, 1),
-    (1, 1, 0), (1, 1, 1), (0, 2, 0), (2, 0, 0), (0, 2, 1), (1, 2, 0),
-    (2, 0, 1), (1, 2, 1), (0, 3, 0), (3, 0, 0), (2, 1, 0), (0, 3, 1),
-    (1, 3, 0), (1, 3, 1), (2, 1, 1), (2, 2, 0), (2, 2, 1), (2, 3, 0),
-    (3, 0, 1), (4, 0, 0), (4, 0, 1), (2, 3, 1), (3, 1, 0), (3, 2, 0),
-    (3, 3, 0), (3, 1, 1), (4, 1, 0), (4, 1, 1), (3, 2, 1), (4, 2, 0),
-    (4, 2, 1), (5, 2, 0), (5, 2, 1), (3, 3, 1), (4, 3, 0), (4, 3, 1),
-    (5, 3, 0), (5, 3, 1),
+    (1, 1, 0), (1, 1, 1), (2, 0, 0), (0, 2, 0), (0, 2, 1), (1, 2, 0),
+    (2, 0, 1), (1, 2, 1), (3, 0, 0), (0, 3, 0), (2, 1, 0), (0, 3, 1),
+    (1, 3, 0), (2, 1, 1), (1, 3, 1), (3, 1, 0), (2, 2, 0), (2, 2, 1),
+    (3, 0, 1), (4, 0, 0), (3, 2, 0), (2, 3, 0), (2, 3, 1), (4, 0, 1),
+    (3, 1, 1), (4, 1, 0), (3, 3, 0), (4, 1, 1), (3, 2, 1), (4, 2, 0),
+    (4, 2, 1), (5, 2, 0), (5, 2, 1), (3, 3, 1), (4, 3, 0), (5, 3, 0),
+    (4, 3, 1), (5, 3, 1),
 )
 
 

time: 73.9 us -> 69.7 us (0.943)
  Pallas kernels: 71.4 us -> 67.1 us
    pallas_call x1, Pallas kernels: 71.4 us -> 67.1 us  [shards(): pl.pallas_call(functools.partial(kernel, sizes), out_shape=jax.ShapeDtype...]
where the time goes in v4:
time: 69.7 us; the launch traced here: 69.3 us
  Pallas kernels  67.1 us (96%)
  local copies, waits for them, and re-layouts  2.26 us (3%)
    pallas_call x1, Pallas kernels, shards(): pl.pallas_call(functools.partial(kernel, sizes), out_shape=jax.ShapeDtype...  67.1 us
    unnamed x1, local copies, waits for them, and re-layouts  2.26 us

profile of v4, /device:TPU:0, one launch (start us, length us, event | category | flops | bytes accessed | tf_op | source)
XLA Modules:
  0.0 69.3 jit_solution(2891603300200936562)
XLA Ops:
  0.0 67.1 %shard_map.55 = bf16[32,128,128]{2,1,0:T(8,128)(2,1)} custom-call(s32[4,64]{1,0:T(4,128)} %bitcast.11, bf16[16,4,128,128]{3,2,1,0:T(8,128)(2,1)} %bitcast.8, bf16[16,4,64,256]{3,2,1,0:T(8,128)(2,1)} %bitcast.9, bf16[4,32,128,256]{3,2,1,0:T(8,128)(2,1)} %bitcast.6, bf16[64,128,128]{2,1,0:T(8,128)(2,1)} %bitcast.10), custom_call_target="tpu_custom_call" | custom-call | tf_op jit(solution)/shard_map/pallas_call | solution.py:302
  67.1 2.3 %copy.7 = bf16[4096,128]{1,0:T(8,128)(2,1)} copy(bf16[4096,128]{1,0:T(8,128)(2,1)} %bitcast.7) | data formatting | bytes 2097152

commit v5 on v4

--- a/solution.py
+++ b/solution.py
@@ -15,8 +15,8 @@
     (1, 1, 0), (1, 1, 1), (2, 0, 0), (0, 2, 0), (0, 2, 1), (1, 2, 0),
     (2, 0, 1), (1, 2, 1), (3, 0, 0), (0, 3, 0), (2, 1, 0), (0, 3, 1),
     (1, 3, 0), (2, 1, 1), (1, 3, 1), (3, 1, 0), (2, 2, 0), (2, 2, 1),
-    (3, 0, 1), (4, 0, 0), (3, 2, 0), (2, 3, 0), (2, 3, 1), (4, 0, 1),
-    (3, 1, 1), (4, 1, 0), (3, 3, 0), (4, 1, 1), (3, 2, 1), (4, 2, 0),
+    (3, 0, 1), (3, 2, 0), (2, 3, 0), (2, 3, 1), (4, 0, 0), (4, 0, 1),
+    (3, 3, 0), (3, 1, 1), (4, 1, 0), (4, 1, 1), (3, 2, 1), (4, 2, 0),
     (4, 2, 1), (5, 2, 0), (5, 2, 1), (3, 3, 1), (4, 3, 0), (5, 3, 0),
     (4, 3, 1), (5, 3, 1),
 )

time: 69.7 us -> 70 us (level)
  no operation moved by 1% of the time
where the time goes in v5:
time: 70 us; the launch traced here: 69.4 us
  Pallas kernels  67.1 us (96%)
  local copies, waits for them, and re-layouts  2.26 us (3%)
    pallas_call x1, Pallas kernels, shards(): pl.pallas_call(functools.partial(kernel, sizes), out_shape=jax.ShapeDtype...  67.1 us
    unnamed x1, local copies, waits for them, and re-layouts  2.26 us

profile of v5, /device:TPU:0, one launch (start us, length us, event | category | flops | bytes accessed | tf_op | source)
XLA Modules:
  0.0 69.4 jit_solution(18279720732138313620)
XLA Ops:
  0.0 67.1 %shard_map.55 = bf16[32,128,128]{2,1,0:T(8,128)(2,1)} custom-call(s32[4,64]{1,0:T(4,128)} %bitcast.11, bf16[16,4,128,128]{3,2,1,0:T(8,128)(2,1)} %bitcast.8, bf16[16,4,64,256]{3,2,1,0:T(8,128)(2,1)} %bitcast.9, bf16[4,32,128,256]{3,2,1,0:T(8,128)(2,1)} %bitcast.6, bf16[64,128,128]{2,1,0:T(8,128)(2,1)} %bitcast.10), custom_call_target="tpu_custom_call" | custom-call | tf_op jit(solution)/shard_map/pallas_call | solution.py:302
  67.1 2.3 %copy.7 = bf16[4096,128]{1,0:T(8,128)(2,1)} copy(bf16[4096,128]{1,0:T(8,128)(2,1)} %bitcast.7) | data formatting | bytes 2097152
